TPU v7x, 32 devices: a whole 2x2x4 slice. The times are simulated.
32 devices in a mesh: expert: 16 (over z, y, core), tensor: 2 (over x).
Axes of the slice: x: 2, y: 2, z: 4, core: 2. Of those that a mesh axis runs over, the one named last changes fastest.
Arguments:
- attn_partial: bfloat16 [2, 256, 3584], P('tensor', 'expert'), may hold values from -4 to 4
- residual_in: bfloat16 [256, 3584], P(('expert', 'tensor')), may hold values from -6 to 6
- norm_gain: bfloat16 [3584], replicated, may hold values from 0.25 to 1.75
- w_in: bfloat16 [16, 3584, 1024], P('expert', None, 'tensor'), may hold values from -0.09375 to 0.09375
- w_out: bfloat16 [16, 1024, 3584], P('expert', 'tensor'), may hold values from -0.375 to 0.375
- routes: int32 [256, 8], P('expert'), may hold values from 0 to 15, all different within a row; in each aligned block of 16 rows (0 to 15, 16 to 31, ...) at most 16 rows name the same one
- gate_weights: float32 [256, 8], P('expert'), may hold values from 0.05 to 0.5
Outputs:
- layer_out: bfloat16 [256, 3584], P('expert')
Inputs may be any that keep to these rules, and one draw needn't show every extreme that they name: `routes`: each row names 8 different experts. In each aligned block of 16 rows (the tokens of one index of expert) no expert is named by more than 16 rows, and in some block an expert is named by exactly 16 rows.
All inputs are finite; a program needn't handle non-finite values.
Results may differ from a plain program's by a relative error of at most 0.02.
Values may be sent and summed in bfloat16 or wider, within the bound.
A program may use at most 64 MiB of HBM per device.

v0:
```python
import jax
import jax.numpy as jnp
from jax import lax
from jax.sharding import PartitionSpec as P

QB = 128


EPSILON = 1e-06


def capacity(group_tokens, top_count, expert_count):
    return min(group_tokens, max(4, 2 * group_tokens * top_count // expert_count))


def shards(attn_partial, residual_in, norm_gain, w_in, w_out, routes, gate_weights):
    group_tokens, top_count = routes.shape
    model_width = residual_in.shape[1]
    expert_count = lax.axis_size("expert")
    slot_count = capacity(group_tokens, top_count, expert_count)
    block_count = model_width // QB
    attention = lax.psum_scatter(
        attn_partial[0].astype(jnp.float32).astype(jnp.bfloat16),
        "tensor",
        scatter_dimension=0,
        tiled=True,
    ).astype(jnp.float32)
    residual = (residual_in.astype(jnp.float32) + attention).astype(jnp.bfloat16)
    stream = residual.astype(jnp.float32)
    rms_value = jnp.sqrt(jnp.mean(stream * stream, axis=1, keepdims=True) + EPSILON)
    normed = stream / rms_value * norm_gain.astype(jnp.float32)
    blocks = normed.reshape(-1, block_count, QB)
    block_scale = (jnp.max(jnp.abs(blocks), axis=2) + EPSILON).astype(jnp.bfloat16)
    quantized = (
        (blocks / block_scale.astype(jnp.float32)[:, :, None])
        .astype(jnp.bfloat16)
        .reshape(-1, model_width)
    )
    group_quant, group_scale, group_resid = (
        lax.all_gather(quantized, "tensor", axis=0, tiled=True),
        lax.all_gather(block_scale, "tensor", axis=0, tiled=True),
        lax.all_gather(residual, "tensor", axis=0, tiled=True),
    )
    pair_expert = routes.reshape(-1)
    onehot = (pair_expert[:, None] == jnp.arange(expert_count, dtype=jnp.int32)[None, :]).astype(
        jnp.int32
    )
    earlier = jnp.cumsum(onehot, axis=0) - onehot
    slot_index = jnp.sum(earlier * onehot, axis=1)
    target = pair_expert * slot_count + slot_index
    pair_total = group_tokens * top_count
    slot_table = (
        jnp.full((expert_count * slot_count,), -1, jnp.int32)
        .at[target]
        .set(jnp.arange(pair_total, dtype=jnp.int32))
    )
    slot_table = slot_table.reshape(expert_count, slot_count)
    filled = slot_table >= 0
    token_ids = jnp.maximum(slot_table, 0) // top_count
    row_block = jnp.where(filled[:, :, None], group_quant[token_ids], jnp.zeros((), jnp.bfloat16))
    scales = jnp.where(filled[:, :, None], group_scale[token_ids], jnp.zeros((), jnp.bfloat16))
    recv_rows, recv_scales = (
        lax.all_to_all(row_block, "expert", split_axis=0, concat_axis=0, tiled=True),
        lax.all_to_all(scales, "expert", split_axis=0, concat_axis=0, tiled=True),
    )
    sources = recv_rows.shape[0]
    widened = recv_rows.reshape(sources, slot_count, block_count, QB).astype(jnp.float32)
    expert_input = (
        (widened * recv_scales.astype(jnp.float32)[:, :, :, None])
        .reshape(sources * slot_count, model_width)
        .astype(jnp.bfloat16)
    )
    hidden = jax.nn.silu(jnp.dot(expert_input, w_in[0], preferred_element_type=jnp.float32)).astype(
        jnp.bfloat16
    )
    partial_value = jnp.dot(hidden, w_out[0], preferred_element_type=jnp.float32).reshape(
        sources, slot_count, model_width
    )
    summed = lax.psum_scatter(
        partial_value.astype(jnp.bfloat16), "tensor", scatter_dimension=2, tiled=True
    )
    returned = lax.all_to_all(summed, "expert", split_axis=0, concat_axis=0, tiled=True)
    quarter = returned.shape[2]
    flat_back = returned.reshape(expert_count * slot_count, quarter)
    picked = flat_back[target].astype(jnp.float32) * gate_weights.reshape(-1)[:, None]
    mixture = jnp.sum(picked.reshape(group_tokens, top_count, quarter), axis=1)
    resid_part = lax.dynamic_slice_in_dim(
        group_resid, lax.axis_index("tensor") * quarter, quarter, 1
    )
    out_part = (resid_part.astype(jnp.float32) + mixture).astype(jnp.bfloat16)
    return lax.all_gather(out_part, "tensor", axis=1, tiled=True)


def solution(mesh):
    return jax.shard_map(
        shards,
        mesh=mesh,
        in_specs=(
            P("tensor", "expert", None),
            P(("expert", "tensor"), None),
            P(),
            P("expert", None, "tensor"),
            P("expert", "tensor", None),
            P("expert", None),
            P("expert", None),
        ),
        out_specs=P("expert", None),
        check_vma=False,
    )
```

profile of v0, /device:TPU:0, one launch (start us, length us, event | category | flops | bytes accessed | tf_op | source)
XLA Modules:
  0.0 172.8 jit_solution(9277905839738415551)
XLA Ops:
  7.3 0.8 copy.17
  9.4 1.0 scatter_custom_fusion
  11.5 10.9 %reduce-scatter.3.cloned.1.call-done = bf16[8,3584]{1,0:T(8,128)(2,1)} async-done(((bf16[16,3584]{1,0:T(8,128)(2,1)}), bf16[8,3584]{1,0:T(8,128)(2,1)}) %reduce-scatter.3.cloned.1.call-update) | async-done | bytes 57360 | tf_op jit(solution)/shard_map/reduce_scatter | solution.py:22
  22.4 1.0 fusion.10
  23.8 4.3 %all_gather.14 = bf16[16,28]{1,0:T(8,128)(2,1)S(1)} all-gather(bf16[8,28]{1,0:T(8,128)(2,1)S(1)} %add_convert_fusion.2), channel_id=1, replica_groups=mesh['expert'=16,'tensor'=2] {'tensor'}, dimensions={0}, use_global_device_ids=true | all-gather | bytes 1344 | tf_op jit(solution)/shard_map/all_gather | solution.py:41
  28.2 4.9 %all_gather.13 = bf16[16,3584]{1,0:T(8,128)(2,1)S(1)} all-gather(bf16[8,3584]{1,0:T(8,128)(2,1)S(1)} %fusion.12), channel_id=1, replica_groups=mesh['expert'=16,'tensor'=2] {'tensor'}, dimensions={0}, use_global_device_ids=true | all-gather | bytes 172032 | tf_op jit(solution)/shard_map/all_gather | solution.py:40
  33.1 1.7 gather_fusion
  34.8 0.9 gather_fusion.1
  36.5 5.6 %all-to-all-start.1 = ((bf16[16,2,224]{2,1,0:T(2,128)(2,1)}), bf16[16,2,224]{2,1,0:T(2,128)(2,1)S(1)}, u32[]{:S(2)}, u32[]{:S(2)}) async-start(bf16[16,2,224]{2,1,0:T(2,128)(2,1)} %reshape.187), calls=%async_computation.2 | async-start | bytes 32768 | tf_op jit(solution)/shard_map/all_to_all | solution.py:64
  42.1 1.4 broadcast_select_fusion
  43.6 5.0 %all-to-all-done.1 = bf16[16,2,224]{2,1,0:T(2,128)(2,1)S(1)} async-done(((bf16[16,2,224]{2,1,0:T(2,128)(2,1)}), bf16[16,2,224]{2,1,0:T(2,128)(2,1)S(1)}, u32[]{:S(2)}, u32[]{:S(2)}) %all-to-all-start.1) | async-done | bytes 14368 | tf_op jit(solution)/shard_map/all_to_all | solution.py:64
  48.6 3.7 %all-to-all-start = ((bf16[16,16,3584]{2,1,0:T(8,128)(2,1)}), bf16[16,16,3584]{2,1,0:T(8,128)(2,1)S(1)}, u32[]{:S(2)}, u32[]{:S(2)}) async-start(bf16[16,16,3584]{2,1,0:T(8,128)(2,1)} %broadcast_select_fusion), calls=%async_computation.1 | async-start | bytes 3670016 | tf_op jit(solution)/shard_map/all_to_all | solution.py:63
  52.5 36.3 %all-to-all-done = bf16[16,16,3584]{2,1,0:T(8,128)(2,1)S(1)} async-done(((bf16[16,16,3584]{2,1,0:T(8,128)(2,1)}), bf16[16,16,3584]{2,1,0:T(8,128)(2,1)S(1)}, u32[]{:S(2)}, u32[]{:S(2)}) %all-to-all-start) | async-done | bytes 1835040 | tf_op jit(solution)/shard_map/all_to_all | solution.py:63
  88.8 2.4 %reshape.148 = f32[16,16,28,128]{3,2,1,0:T(8,128)} reshape(bf16[16,16,3584]{2,1,0:T(8,128)(2,1)S(1)} %all-to-all-done) | data formatting | bytes 5505024 | tf_op jit(solution)/shard_map/convert_element_type | solution.py:67
  91.2 3.0 %multiply_convert_fusion = bf16[16,16,28,128]{3,2,1,0:T(8,128)(2,1)S(1)} fusion(f32[16,16,28,128]{3,2,1,0:T(8,128)} %reshape.148, f32[16,16,28]{2,1,0:T(8,128)S(1)} %convert_element_type.98), kind=kLoop, calls=%fused_computation.5 | loop fusion | flops 1835008 | bytes 5533696 | tf_op jit(solution)/shard_map/convert_element_type | solution.py:71
  94.5 1.2 multiply_convert_fusion.1
  95.7 0.8 copy-done.2
  96.5 2.4 %convolution_convert_fusion = bf16[16,16,3584]{2,1,0:T(8,128)(2,1)} fusion(bf16[16,16,512]{2,1,0:T(8,128)(2,1)S(1)} %bitcast.44, bf16[1,512,3584]{2,1,0:T(8,128)(2,1)S(1)} %copy-done.2), kind=kOutput, calls=%fused_computation.4 | convolution fusion | flops 940441600 | bytes 5767168 | tf_op jit(solution)/shard_map/dot_general | solution.py:76
  98.9 33.6 %reduce-scatter.5.cloned.1.call-done = bf16[16,16,1792]{2,1,0:T(8,128)(2,1)} async-done(((bf16[16,16,3584]{2,1,0:T(8,128)(2,1)}), bf16[16,16,1792]{2,1,0:T(8,128)(2,1)}) %reduce-scatter.5.cloned.1.call-update) | async-done | bytes 917520 | tf_op jit(solution)/shard_map/reduce_scatter | solution.py:79
  132.6 5.6 %all-to-all-start.2 = ((bf16[16,16,1792]{2,1,0:T(8,128)(2,1)}), bf16[16,16,1792]{2,1,0:T(8,128)(2,1)S(1)}, u32[]{:S(2)}, u32[]{:S(2)}) async-start(bf16[16,16,1792]{2,1,0:T(8,128)(2,1)} %reduce-scatter.5.cloned.1.call-done), calls=%async_computation.4 | async-start | bytes 1835008 | tf_op jit(solution)/shard_map/all_to_all | solution.py:82
  138.3 4.9 %all_gather.12 = bf16[16,3584]{1,0:T(8,128)(2,1)S(1)} all-gather(bf16[8,3584]{1,0:T(8,128)(2,1)S(1)} %get-tuple-element.6), channel_id=1, replica_groups=mesh['expert'=16,'tensor'=2] {'tensor'}, dimensions={0}, use_global_device_ids=true | all-gather | bytes 172032 | tf_op jit(solution)/shard_map/all_gather | solution.py:42
  143.2 15.8 %all-to-all-done.2 = bf16[16,16,1792]{2,1,0:T(8,128)(2,1)S(1)} async-done(((bf16[16,16,1792]{2,1,0:T(8,128)(2,1)}), bf16[16,16,1792]{2,1,0:T(8,128)(2,1)S(1)}, u32[]{:S(2)}, u32[]{:S(2)}) %all-to-all-start.2) | async-done | bytes 917536 | tf_op jit(solution)/shard_map/all_to_all | solution.py:82
  159.0 0.9 gather_fusion.2
  160.4 4.9 %all_gather.15 = bf16[16,3584]{1,0:T(8,128)(2,1)S(1)} all-gather(bf16[16,1792]{1,0:T(8,128)(2,1)S(1)} %add_convert_fusion), channel_id=1, replica_groups=mesh['expert'=16,'tensor'=2] {'tensor'}, dimensions={1}, use_global_device_ids=true | all-gather | bytes 172032 | tf_op jit(solution)/shard_map/all_gather | solution.py:91
  (42 shorter events, 6.1 us)
Async XLA Ops:
  6.5 15.9 %reduce-scatter.3.cloned.1.call-start = ((), (), s32[]{:S(2)}) async-start(), calls=%async_computation.5 | async-start | bytes 172032 | tf_op jit(solution)/shard_map/reduce_scatter | solution.py:22
  36.5 12.1 %all-to-all-start.1 = ((bf16[16,2,224]{2,1,0:T(2,128)(2,1)}), bf16[16,2,224]{2,1,0:T(2,128)(2,1)S(1)}, u32[]{:S(2)}, u32[]{:S(2)}) async-start(bf16[16,2,224]{2,1,0:T(2,128)(2,1)} %reshape.187), calls=%async_computation.2 | async-start | bytes 32768 | tf_op jit(solution)/shard_map/all_to_all | solution.py:64
  48.6 40.2 %all-to-all-start = ((bf16[16,16,3584]{2,1,0:T(8,128)(2,1)}), bf16[16,16,3584]{2,1,0:T(8,128)(2,1)S(1)}, u32[]{:S(2)}, u32[]{:S(2)}) async-start(bf16[16,16,3584]{2,1,0:T(8,128)(2,1)} %broadcast_select_fusion), calls=%async_computation.1 | async-start | bytes 3670016 | tf_op jit(solution)/shard_map/all_to_all | solution.py:63
  52.4 80.2 %reduce-scatter.5.cloned.1.call-start = ((), (), s32[]{:S(2)}) async-start(), calls=%async_computation.6 | async-start | bytes 2752512 | tf_op jit(solution)/shard_map/reduce_scatter | solution.py:79
  91.2 3.3 %copy-start.1 = (bf16[1,3584,512]{2,1,0:T(8,128)(2,1)S(1)}, bf16[1,3584,512]{2,1,0:T(8,128)(2,1)}, u32[]{:S(2)}) copy-start(bf16[1,3584,512]{2,1,0:T(8,128)(2,1)} %param.10) | copy-start | bytes 11010052
  94.5 2.0 %copy-start.2 = (bf16[1,512,3584]{2,1,0:T(8,128)(2,1)S(1)}, bf16[1,512,3584]{2,1,0:T(8,128)(2,1)}, u32[]{:S(2)}) copy-start(bf16[1,512,3584]{2,1,0:T(8,128)(2,1)} %param.11) | copy-start | bytes 11010052
  98.9 39.3 %copy-start = (f32[16,8]{0,1:T(8,128)S(1)}, f32[16,8]{0,1:T(8,128)}, u32[]{:S(2)}) copy-start(f32[16,8]{0,1:T(8,128)} %param.13) | copy-start | bytes 1540
  132.6 26.4 %all-to-all-start.2 = ((bf16[16,16,1792]{2,1,0:T(8,128)(2,1)}), bf16[16,16,1792]{2,1,0:T(8,128)(2,1)S(1)}, u32[]{:S(2)}, u32[]{:S(2)}) async-start(bf16[16,16,1792]{2,1,0:T(8,128)(2,1)} %reduce-scatter.5.cloned.1.call-done), calls=%async_computation.4 | async-start | bytes 1835008 | tf_op jit(solution)/shard_map/all_to_all | solution.py:82
Sparse Core Ops, SparseCore 0:
  9.6 12.7 reduce-scatter.2
  99.1 33.4 reduce-scatter.4
where the time goes:
time: 174 us; the launch traced here: 173 us
  waiting for transfers between devices  102 us (59%)
  blocking collectives  19 us (11%)
  starting transfers between devices  15 us (9%)
  between operations  13.6 us (8%)
  local copies, waits for them, and re-layouts  11 us (6%)
  other arithmetic  8.18 us (5%)
  matrix products  3.6 us (2%)
    all_to_all x1, waiting for transfers between devices, shards(): lax.all_to_all(row_block, 'expert', split_axis=0, concat_axis=0, tiled=True)  36.3 us
    reduce_scatter x1, waiting for transfers between devices, shards(): lax.psum_scatter(partial_value.astype(jnp.bfloat16), 'tensor', scatter_di...  33.6 us
    all_to_all x1, waiting for transfers between devices, shards(): lax.all_to_all(summed, 'expert', split_axis=0, concat_axis=0, tiled=True)  15.8 us
    reduce_scatter x1, waiting for transfers between devices, shards(): lax.psum_scatter(attn_partial[0].astype(jnp.float32).astype(jnp.bfloat16)...  10.9 us
    all_to_all x1, starting transfers between devices, shards(): lax.all_to_all(summed, 'expert', split_axis=0, concat_axis=0, tiled=True)  5.63 us
    all_to_all x1, starting transfers between devices, shards(): lax.all_to_all(scales, 'expert', split_axis=0, concat_axis=0, tiled=True)  5.62 us
    all_to_all x1, waiting for transfers between devices, shards(): lax.all_to_all(scales, 'expert', split_axis=0, concat_axis=0, tiled=True)  5.05 us
    all_gather x1, blocking collectives, shards(): return lax.all_gather(out_part, 'tensor', axis=1, tiled=True)  4.93 us
  transfers between devices with their start and end apart: 5, of which 5 were waited for; matrix products, arithmetic and copies ran while one was open for 3% of the time, Pallas kernels for 0%

commit v1 on v0

--- a/solution.py
+++ b/solution.py
@@ -13,12 +13,70 @@
     return min(group_tokens, max(4, 2 * group_tokens * top_count // expert_count))
 
 
+def own_rows(attention, residual_in, norm_gain):
+    model_width = residual_in.shape[1]
+    block_count = model_width // QB
+    residual = (residual_in.astype(jnp.float32) + attention).astype(jnp.bfloat16)
+    stream = residual.astype(jnp.float32)
+    rms_value = jnp.sqrt(jnp.mean(stream * stream, axis=1, keepdims=True) + EPSILON)
+    normed = stream / rms_value * norm_gain.astype(jnp.float32)
+    blocks = normed.reshape(-1, block_count, QB)
+    block_scale = (jnp.max(jnp.abs(blocks), axis=2) + EPSILON).astype(jnp.bfloat16)
+    wide = block_scale.astype(jnp.float32)[:, :, None]
+    quantized = (blocks / wide).astype(jnp.bfloat16)
+    expert_input = (quantized.astype(jnp.float32) * wide).astype(jnp.bfloat16)
+    return residual, expert_input.reshape(-1, model_width)
+
+
+def dense_gates(routes, gate_weights, expert_count):
+    chosen = routes[:, :, None] == jnp.arange(expert_count, dtype=jnp.int32)
+    return jnp.sum(jnp.where(chosen, gate_weights[:, :, None], 0.0), axis=1)
+
+
+def dense_shards(attn_partial, residual_in, norm_gain, w_in, w_out, routes, gate_weights):
+    model_width = residual_in.shape[1]
+    expert_count = lax.axis_size("expert")
+    attention = lax.psum_scatter(
+        attn_partial[0], "tensor", scatter_dimension=0, tiled=True
+    ).astype(jnp.float32)
+    residual, expert_input = own_rows(attention, residual_in, norm_gain)
+    own_count = residual.shape[0]
+    gates = dense_gates(routes, gate_weights, expert_count)
+    gates = lax.dynamic_slice_in_dim(gates, lax.axis_index("tensor") * own_count, own_count, 0)
+    high = gates.astype(jnp.bfloat16)
+    middle = (gates - high.astype(jnp.float32)).astype(jnp.bfloat16)
+    rest = gates - high.astype(jnp.float32) - middle.astype(jnp.float32)
+    pieces = jnp.concatenate([high, middle, rest.astype(jnp.bfloat16)], axis=1)
+    pieces = jnp.pad(pieces, ((0, 0), (0, QB - pieces.shape[1])))
+    packed = jnp.concatenate([expert_input, pieces], axis=1)
+    everything = lax.all_gather(packed, ("expert", "tensor"), axis=0, tiled=True)
+    rows, codes = everything[:, :model_width], everything[:, model_width:]
+    mine = lax.axis_index("expert")
+    lane = jnp.arange(QB, dtype=jnp.int32)[None, :]
+    own_lane = (lane < 3 * expert_count) & (lane % expert_count == mine)
+    gate = jnp.sum(jnp.where(own_lane, codes.astype(jnp.float32), 0.0), axis=1, keepdims=True)
+    hidden = jax.nn.silu(jnp.dot(rows, w_in[0], preferred_element_type=jnp.float32)).astype(
+        jnp.bfloat16
+    )
+    partial_value = jnp.dot(hidden, w_out[0], preferred_element_type=jnp.float32)
+    weighted = (partial_value * gate).astype(jnp.bfloat16)
+    mixture = lax.psum_scatter(
+        weighted, ("expert", "tensor"), scatter_dimension=0, tiled=True
+    ).astype(jnp.float32)
+    out_part = (residual.astype(jnp.float32) + mixture).astype(jnp.bfloat16)
+    return lax.all_gather(out_part, "tensor", axis=0, tiled=True)
+
+
 def shards(attn_partial, residual_in, norm_gain, w_in, w_out, routes, gate_weights):
     group_tokens, top_count = routes.shape
     model_width = residual_in.shape[1]
     expert_count = lax.axis_size("expert")
     slot_count = capacity(group_tokens, top_count, expert_count)
     block_count = model_width // QB
+    if slot_count == group_tokens:
+        return dense_shards(
+            attn_partial, residual_in, norm_gain, w_in, w_out, routes, gate_weights
+        )
     attention = lax.psum_scatter(
         attn_partial[0].astype(jnp.float32).astype(jnp.bfloat16),
         "tensor",
@@ -42,11 +100,9 @@
         lax.all_gather(residual, "tensor", axis=0, tiled=True),
     )
     pair_expert = routes.reshape(-1)
-    onehot = (pair_expert[:, None] == jnp.arange(expert_count, dtype=jnp.int32)[None, :]).astype(
-        jnp.int32
-    )
-    earlier = jnp.cumsum(onehot, axis=0) - onehot
-    slot_index = jnp.sum(earlier * onehot, axis=1)
+    order = jnp.arange(pair_expert.shape[0], dtype=jnp.int32)
+    before = (pair_expert[:, None] == pair_expert[None, :]) & (order[None, :] < order[:, None])
+    slot_index = jnp.sum(before.astype(jnp.int32), axis=1)
     target = pair_expert * slot_count + slot_index
     pair_total = group_tokens * top_count
     slot_table = (

time: 174 us -> 239 us (1.37)
  waiting for transfers between devices: 102 us -> 207 us
  starting transfers between devices: 15 us -> 0.08 us
  blocking collectives: 19 us -> 4.85 us
  local copies, waits for them, and re-layouts: 11 us -> 2.16 us
  other arithmetic: 8.18 us -> 4.61 us
  matrix products: 3.6 us -> 7.16 us
    reduce_scatter x2, waiting for transfers between devices: 44.5 us -> 149 us  [the longest x1 136 us: dense_shards(): lax.psum_scatter(weighted, ('expert', 'tensor'), scatter_dimension=0, til...]
    all_to_all x3 -> x0, waiting for transfers between devices: 57.1 us -> none  [the longest x1 36.3 us: shards(): lax.all_to_all(row_block, 'expert', split_axis=0, concat_axis=0, tiled=True)]
    all_gather x0 -> x1, waiting for transfers between devices: none -> 57.1 us  [dense_shards(): lax.all_gather(packed, ('expert', 'tensor'), axis=0, tiled=True)]
    all_to_all x3 -> x0, starting transfers between devices: 15 us -> none  [the longest x1 5.63 us: shards(): lax.all_to_all(summed, 'expert', split_axis=0, concat_axis=0, tiled=True)]
    all_gather x4 -> x1, blocking collectives: 19 us -> 4.85 us  [dense_shards(): return lax.all_gather(out_part, 'tensor', axis=0, tiled=True)]
    dot_general x2 -> x1, matrix products: 3.6 us -> 7.16 us  [dense_shards(): jnp.dot(hidden, w_out[0], preferred_element_type=jnp.float32)]
    gather x3 -> x0, local copies, waits for them, and re-layouts: 3.5 us -> none  [the longest x1 1.71 us: shards(): group_quant[token_ids]]
    convert_element_type x2 -> x0, local copies, waits for them, and re-layouts: 2.47 us -> none  [the longest x1 2.38 us: shards(): recv_rows.reshape(sources, slot_count, block_count, QB).astype(jnp.float32)]
  transfers between devices with their start and end apart: 5 -> 3, of which waited for: 5 -> 3; matrix products, arithmetic and copies ran while one was open for 3% -> 1% of each run, Pallas kernels for 0% -> 0%
where the time goes in v1:
time: 239 us
  waiting for transfers between devices  207 us (87%)
  between operations  13.2 us (6%)
  matrix products  7.16 us (3%)
  blocking collectives  4.85 us (2%)
  other arithmetic  4.61 us (2%)
    reduce_scatter x1, waiting for transfers between devices, dense_shards(): lax.psum_scatter(weighted, ('expert', 'tensor'), scatter_dimension=0, til...  136 us
    all_gather x1, waiting for transfers between devices, dense_shards(): lax.all_gather(packed, ('expert', 'tensor'), axis=0, tiled=True)  57.1 us
    reduce_scatter x1, waiting for transfers between devices, dense_shards(): lax.psum_scatter(attn_partial[0], 'tensor', scatter_dimension=0, tiled=True)  12.7 us
    dot_general x1, matrix products, dense_shards(): jnp.dot(hidden, w_out[0], preferred_element_type=jnp.float32)  7.16 us
    all_gather x1, blocking collectives, dense_shards(): return lax.all_gather(out_part, 'tensor', axis=0, tiled=True)  4.85 us
  transfers between devices with their start and end apart: 3, of which 3 were waited for; matrix products, arithmetic and copies ran while one was open for 1% of the time, Pallas kernels for 0%

profile of v1, /device:TPU:0, one launch (start us, length us, event | category | flops | bytes accessed | tf_op | source)
XLA Modules:
  0.0 238.8 jit_solution(15412379204777568517)
XLA Ops:
  6.5 0.0 reduce-scatter.3.cloned.1.call-start
  6.5 0.7 reduce-scatter.3.cloned.1.call-update
  7.3 0.0 all-gather.2.cloned.1.call-start
  7.3 0.8 copy.10
  8.1 0.8 copy.11
  8.8 0.1 select_reduce_fusion.1
  8.9 0.7 convert_element_type.79
  9.6 0.1 fusion.25
  9.7 12.7 %reduce-scatter.3.cloned.1.call-done = bf16[8,3584]{1,0:T(8,128)(2,1)} async-done(((bf16[16,3584]{1,0:T(8,128)(2,1)}), bf16[8,3584]{1,0:T(8,128)(2,1)}) %reduce-scatter.3.cloned.1.call-update) | async-done | bytes 57360 | tf_op jit(solution)/shard_map/reduce_scatter | solution.py:39
  22.4 1.0 fusion.14
  23.4 0.2 bitcast_reduce_fusion
  23.6 0.1 fusion.18
  23.7 0.6 pad_maximum_fusion
  24.4 0.0 all-gather.2.cloned.1.call-update
  24.4 0.0 reduce-scatter.5.cloned.1.call-start
  24.5 57.1 %all-gather.2.cloned.1.call-done = bf16[256,3712]{1,0:T(8,128)(2,1)} async-done(((bf16[8,3712]{1,0:T(8,128)(2,1)}), bf16[256,3712]{1,0:T(8,128)(2,1)}) %all-gather.2.cloned.1.call-update) | async-done | bytes 1900560 | tf_op jit(solution)/shard_map/all_gather | solution.py:52
  81.6 0.9 select_reduce_fusion
  82.5 7.2 %fusion = bf16[256,3584]{1,0:T(8,128)(2,1)} fusion(bf16[1,512,3584]{2,1,0:T(8,128)(2,1)} %param.11, f32[256]{0:T(256)S(1)} %select_reduce_fusion, bf16[1,3584,512]{2,1,0:T(8,128)(2,1)} %param.10, bf16[256,3712]{1,0:T(8,128)(2,1)} %all-gather.2.cloned.1.call-done), kind=kOutput, calls=%fused_computation.1 | convolution fusion | flops 1881538560 | bytes 11011072 | tf_op jit(solution)/shard_map/dot_general | solution.py:61
  89.7 0.0 reduce-scatter.5.cloned.1.call-update
  89.7 136.3 %reduce-scatter.5.cloned.1.call-done = bf16[8,3584]{1,0:T(8,128)(2,1)} async-done(((bf16[256,3584]{1,0:T(8,128)(2,1)}), bf16[8,3584]{1,0:T(8,128)(2,1)}) %reduce-scatter.5.cloned.1.call-update) | async-done | bytes 57360 | tf_op jit(solution)/shard_map/reduce_scatter | solution.py:63
  226.0 0.8 fusion.16
  226.8 4.9 %all_gather.7 = bf16[16,3584]{1,0:T(8,128)(2,1)S(1)} all-gather(bf16[8,3584]{1,0:T(8,128)(2,1)S(1)} %fusion.16), channel_id=1, replica_groups=mesh['expert'=16,'tensor'=2] {'tensor'}, dimensions={0}, use_global_device_ids=true | all-gather | bytes 172032 | tf_op jit(solution)/shard_map/all_gather | solution.py:67
  231.7 0.6 copy.13
  (4 shorter events, 0.0 us)
Async XLA Ops:
  6.5 15.9 %reduce-scatter.3.cloned.1.call-start = ((), (), s32[]{:S(2)}) async-start(), calls=%async_computation.2 | async-start | bytes 172032 | tf_op jit(solution)/shard_map/reduce_scatter | solution.py:39
  7.3 74.3 %all-gather.2.cloned.1.call-start = ((), (), s32[]{:S(2)}) async-start(), calls=%async_computation.3 | async-start | bytes 1959936 | tf_op jit(solution)/shard_map/all_gather | solution.py:52
  24.4 201.6 %reduce-scatter.5.cloned.1.call-start = ((), (), s32[]{:S(2)}) async-start(), calls=%async_computation.4 | async-start | bytes 1892352 | tf_op jit(solution)/shard_map/reduce_scatter | solution.py:63
Sparse Core Ops, SparseCore 0:
  9.6 12.7 reduce-scatter.2
  25.3 56.1 all-gather.1
  89.8 136.1 reduce-scatter.4
